TPU v7x, 256 devices: a whole 4x4x8 slice. The times are simulated.
256 devices in a mesh: orb: 16 (over z, core), slab: 16 (over y, x).
Axes of the slice: x: 4, y: 4, z: 8, core: 2. Of those that a mesh axis runs over, the one named last changes fastest.
Arguments:
- orbitals: float32 [16, 128, 48, 128], P('orb', 'slab'), may hold values from -6 to 6
- occupations: float32 [16], P('orb'), may hold values from 0.25 to 1
Outputs:
- exchange: float32 [16, 128, 48, 128], P('orb', 'slab')
All inputs are finite; a program needn't handle non-finite values.
Results may differ from a plain program's by a relative error of at most 0.0003.
Values sent between devices are 32-bit elements; how exact they have to be, the bound alone decides.
A program may use at most 128 MiB of HBM per device.

v0:
```python
import jax
import jax.numpy as jnp
from jax import lax
from jax.sharding import PartitionSpec as P

CYCLES = 2
LEVELS = 3
SWEEPS = 6


screening = 0.001
relaxation = 0.8


def with_halo(cells, sides, width):
    for axis, dim in sides:
        count = lax.axis_size(axis)
        ends = count - 1
        head = lax.slice_in_dim(cells, 0, width, axis=dim)
        tail = lax.slice_in_dim(cells, cells.shape[dim] - width, cells.shape[dim], axis=dim)
        cells = jnp.concatenate(
            [
                lax.ppermute(tail, axis, [(i, (i + 1) % count) for i in range(ends)]),
                cells,
                lax.ppermute(head, axis, [((i + 1) % count, i) for i in range(ends)]),
            ],
            axis=dim,
        )
    return cells


def shifted(shard, axis, by):
    peers = lax.axis_size(axis)
    return lax.ppermute(shard, axis, [(i, (i + by) % peers) for i in range(peers)])


def combine_sides(padded, values, inverse_step):
    beside = padded[:, 2:] + padded[:, :-2]
    beside = beside + jnp.roll(values, 1, 2) + jnp.roll(values, -1, 2)
    beside = beside + jnp.roll(values, 1, 3) + jnp.roll(values, -1, 3)
    return (6.0 * inverse_step + screening) * values - inverse_step * beside


def operate(values, inverse_step):
    padded = with_halo(values, (("slab", 1),), 1)
    return combine_sides(padded, values, inverse_step)


def operate_coarse(values, inverse_step):
    padded = with_halo(values, (("slab", 1),), 1)
    return combine_sides(padded, values, inverse_step)


def relax_with(values, applied, source, inverse_step):
    return values + relaxation * (source - applied) / (6.0 * inverse_step + screening)


def restrict(values):
    shape = values.shape
    grouped = values.reshape(shape[0], shape[1] // 2, 2, shape[2] // 2, 2, shape[3] // 2, 2)
    return jnp.sum(grouped, axis=(2, 4, 6)) * 0.125


def prolong(values):
    return jnp.repeat(jnp.repeat(jnp.repeat(values, 2, 1), 2, 2), 2, 3)


def coarse_solve(source, inverse_step):
    iterate = jnp.zeros_like(source)
    for sweep_index in range(SWEEPS):
        iterate = relax_with(iterate, operate_coarse(iterate, inverse_step), source, inverse_step)
    return iterate


def vcycle(values, source, level_index):
    inverse_step = 0.25**level_index
    if level_index == LEVELS:
        return coarse_solve(source, inverse_step)
    iterate = relax_with(values, operate(values, inverse_step), source, inverse_step)
    residual = source - operate(iterate, inverse_step)
    coarse_source = restrict(residual)
    correction = vcycle(jnp.zeros_like(coarse_source), coarse_source, level_index + 1)
    iterate = iterate + prolong(correction)
    return relax_with(iterate, operate(iterate, inverse_step), source, inverse_step)


def solve(source):
    iterate = jnp.zeros_like(source)
    for cycle_index in range(CYCLES):
        iterate = vcycle(iterate, source, 0)
    return iterate


def on_device(orbitals, occupations):
    count = orbitals.shape[0]
    left_orbs, left_occ = shifted((orbitals, occupations), "orb", 1)
    right_orbs, right_occ = shifted((orbitals, occupations), "orb", -1)
    visiting = jnp.stack([left_orbs, right_orbs])
    weights = jnp.stack([left_occ, right_occ])
    density = orbitals[None, :, None] * visiting[:, None, :]
    shape = density.shape
    potential = solve(density.reshape((2 * count * count,) + shape[3:])).reshape(shape)
    weighted = visiting * weights[:, :, None, None, None]
    return -jnp.sum(potential * weighted[:, None], axis=(0, 2))


def solution(mesh):
    return jax.shard_map(
        on_device,
        mesh=mesh,
        in_specs=(P("orb", "slab", None, None), P("orb")),
        out_specs=P("orb", "slab", None, None),
        check_vma=False,
    )
```

profile of v0, /device:TPU:24, one launch (start us, length us, event | category | flops | bytes accessed | tf_op | source)
XLA Modules:
  0.0 394.3 jit_solution(12764378822184033394)
XLA Ops:
  0.0 5.3 %collective-permute-start.1 = (f32[1,8,48,128]{3,2,1,0:T(8,128)}, f32[1,8,48,128]{3,2,1,0:T(8,128)S(1)}, u32[]{:S(2)}, u32[]{:S(2)}) collective-permute-start(f32[1,8,48,128]{3,2,1,0:T(8,128)} %param.2), channel_id=1, source_target_pairs={{0,240},{16,0},{32,16},{48,32},{64,48},{80,64},{96,80},{112,96},{1... | collective-permute-start | bytes 589832 | tf_op jit(solution)/shard_map/ppermute | solution.py:34
  5.4 4.8 %collective-permute-start.2 = (f32[2,1,48,128]{2,1,3,0:T(1,128)S(1)}, f32[2,1,48,128]{2,1,3,0:T(1,128)S(1)}, u32[]{:S(2)}, u32[]{:S(2)}) collective-permute-start(f32[2,1,48,128]{2,1,3,0:T(1,128)S(1)} %broadcast.246), channel_id=1, source_target_pairs={{1,0},{2,1},{3,2},{4,3},{5,4},{6,5},{7,6},{8,7},{9,8},{10,9},{11,1... | collective-permute-start | bytes 147464 | tf_op jit(solution)/shard_map/ppermute | solution.py:25
  21.8 6.0 %collective-permute-start.6 = (f32[2,1,24,64]{3,2,1,0:T(8,128)}, f32[2,1,24,64]{3,2,1,0:T(8,128)}, u32[]{:S(2)}, u32[]{:S(2)}) collective-permute-start(f32[2,1,24,64]{3,2,1,0:T(8,128)} %broadcast.249), channel_id=1, source_target_pairs={{1,0},{2,1},{3,2},{4,3},{5,4},{6,5},{7,6},{8,7},{9,8},{10,9},{11,1... | collective-permute-start | bytes 36872 | tf_op jit(solution)/shard_map/ppermute | solution.py:25
  32.2 6.0 %collective-permute-start.10 = (f32[2,1,12,32]{3,2,1,0:T(8,128)}, f32[2,1,12,32]{3,2,1,0:T(8,128)}, u32[]{:S(2)}, u32[]{:S(2)}) collective-permute-start(f32[2,1,12,32]{3,2,1,0:T(8,128)} %broadcast.253), channel_id=1, source_target_pairs={{1,0},{2,1},{3,2},{4,3},{5,4},{6,5},{7,6},{8,7},{9,8},{10,9},{11,1... | collective-permute-start | bytes 9224 | tf_op jit(solution)/shard_map/ppermute | solution.py:25
  47.7 3.9 collective-permute-start.5
  61.0 5.2 %fusion.47 = f32[2,8,48,128]{2,1,3,0:T(8,128)} fusion(f32[2,8,48,128]{2,1,3,0:T(8,128)S(1)} %get-tuple-element.11, f32[2,1,48,128]{2,1,3,0:T(1,128)} %collective-permute-done.5, f32[2,1,48,128]{2,1,3,0:T(1,128)S(1)} %collective-permute-done.4, f32[2,8,47,128]{2,1,3,0:T(8,128)} %get-tuple-element.58, f32[2,8,1,128]{2,1,3,0:T(8,128)} %get-tuple-element.60, ...), kind=kLoop, calls=%fused_computation.58 | loop fusion | flops 1474560 | bytes 3440640 | tf_op jit(solution)/shard_map/sub | solution.py:80
  67.8 26.6 %reshape.131 = f32[2,4,2,24,2,64,2]{6,5,4,3,2,1,0:T(8,128)} reshape(f32[2,8,48,128]{3,2,1,0:T(8,128)S(1)} %copy.143) | data formatting | bytes 786432 | tf_op jit(solution)/shard_map/reshape | solution.py:60
  94.3 9.4 %reduce_sum.77 = f32[2,4,24,64]{3,2,1,0:T(8,128)S(1)} reduce(f32[2,4,2,24,2,64,2]{6,5,4,3,2,1,0:T(8,128)} %reshape.131, f32[]{:T(128)} %constant.101.clone.1), dimensions={2,4,6}, to_apply=%region_0.1 | reduce | flops 86016 | bytes 442372 | tf_op jit(solution)/shard_map/reduce_sum | solution.py:61
  106.8 3.9 collective-permute-start.9
  114.8 5.0 %reshape.132 = f32[2,2,2,12,2,32,2]{6,5,4,3,2,1,0:T(8,128)} reshape(f32[2,4,24,64]{3,2,1,0:T(8,128)S(1)} %fusion.88) | data formatting | bytes 98304 | tf_op jit(solution)/shard_map/reshape | solution.py:60
  123.0 4.1 %collective-permute-start.12 = (f32[2,1,12,32]{3,2,1,0:T(8,128)S(1)}, f32[2,1,12,32]{3,2,1,0:T(8,128)S(1)}, u32[]{:S(2)}, u32[]{:S(2)}) collective-permute-start(f32[2,1,12,32]{3,2,1,0:T(8,128)S(1)} %get-tuple-element.141), channel_id=1, source_target_pairs={{1,0},{2,1},{3,2},{4,3},{5,4},{6,5},{7,6},{8,7},{9,8},{10,9},{11,1... | collective-permute-start | bytes 9224 | tf_op jit(solution)/shard_map/ppermute | solution.py:25
  129.1 5.8 %collective-permute-done.13 = f32[2,1,12,32]{3,2,1,0:T(8,128)S(1)} collective-permute-done((f32[2,1,12,32]{3,2,1,0:T(8,128)S(1)}, f32[2,1,12,32]{3,2,1,0:T(8,128)S(1)}, u32[]{:S(2)}, u32[]{:S(2)}) %collective-permute-start.13) | collective-permute-done | bytes 3104 | tf_op jit(solution)/shard_map/ppermute | solution.py:23
  137.3 3.9 collective-permute-start.17
  147.0 3.9 collective-permute-start.19
  156.6 3.9 collective-permute-start.21
  166.3 3.9 collective-permute-start.23
  175.9 3.9 collective-permute-start.25
  186.0 3.9 collective-permute-start.27
  196.5 4.1 %collective-permute-start.29 = (f32[2,1,24,64]{3,2,1,0:T(8,128)S(1)}, f32[2,1,24,64]{3,2,1,0:T(8,128)S(1)}, u32[]{:S(2)}, u32[]{:S(2)}) collective-permute-start(f32[2,1,24,64]{3,2,1,0:T(8,128)S(1)} %get-tuple-element.92), channel_id=1, source_target_pairs={{0,1},{1,2},{2,3},{3,4},{4,5},{5,6},{6,7},{7,8},{8,9},{9,10},{10,1... | collective-permute-start | bytes 36872 | tf_op jit(solution)/shard_map/ppermute | solution.py:23
  208.0 3.9 collective-permute-start.31
  212.9 4.0 %collective-permute-done.31 = f32[2,1,48,128]{2,1,3,0:T(1,128)S(1)} collective-permute-done((f32[2,1,48,128]{2,1,3,0:T(1,128)S(1)}, f32[2,1,48,128]{2,1,3,0:T(1,128)S(1)}, u32[]{:S(2)}, u32[]{:S(2)}) %collective-permute-start.31) | collective-permute-done | bytes 49184 | tf_op jit(solution)/shard_map/ppermute | solution.py:23
  221.2 3.9 collective-permute-start.33
  226.1 4.0 %collective-permute-done.33 = f32[2,1,48,128]{2,1,3,0:T(1,128)S(1)} collective-permute-done((f32[2,1,48,128]{2,1,3,0:T(1,128)S(1)}, f32[2,1,48,128]{2,1,3,0:T(1,128)S(1)}, u32[]{:S(2)}, u32[]{:S(2)}) %collective-permute-start.33) | collective-permute-done | bytes 49184 | tf_op jit(solution)/shard_map/ppermute | solution.py:23
  234.3 3.9 collective-permute-start.35
  239.3 4.0 %collective-permute-done.35 = f32[2,1,48,128]{2,1,3,0:T(1,128)S(1)} collective-permute-done((f32[2,1,48,128]{2,1,3,0:T(1,128)S(1)}, f32[2,1,48,128]{2,1,3,0:T(1,128)S(1)}, u32[]{:S(2)}, u32[]{:S(2)}) %collective-permute-start.35) | collective-permute-done | bytes 49184 | tf_op jit(solution)/shard_map/ppermute | solution.py:23
  247.0 26.6 %reshape.139 = f32[2,4,2,24,2,64,2]{6,5,4,3,2,1,0:T(8,128)} reshape(f32[2,8,48,128]{3,2,1,0:T(8,128)S(1)} %copy.151) | data formatting | bytes 786432 | tf_op jit(solution)/shard_map/reshape | solution.py:60
  273.5 9.5 %reduce_sum.82 = f32[2,4,24,64]{3,2,1,0:T(8,128)S(1)} reduce(f32[2,4,2,24,2,64,2]{6,5,4,3,2,1,0:T(8,128)} %reshape.139, f32[]{:T(128)} %constant.101.clone.1), dimensions={2,4,6}, to_apply=%region_4.5 | reduce | flops 86016 | bytes 442372 | tf_op jit(solution)/shard_map/reduce_sum | solution.py:61
  285.2 4.1 %collective-permute-start.37 = (f32[2,1,24,64]{3,2,1,0:T(8,128)S(1)}, f32[2,1,24,64]{3,2,1,0:T(8,128)S(1)}, u32[]{:S(2)}, u32[]{:S(2)}) collective-permute-start(f32[2,1,24,64]{3,2,1,0:T(8,128)S(1)} %get-tuple-element.82), channel_id=1, source_target_pairs={{0,1},{1,2},{2,3},{3,4},{4,5},{5,6},{6,7},{7,8},{8,9},{9,10},{10,1... | collective-permute-start | bytes 36872 | tf_op jit(solution)/shard_map/ppermute | solution.py:23
  293.2 5.0 %reshape.140 = f32[2,2,2,12,2,32,2]{6,5,4,3,2,1,0:T(8,128)} reshape(f32[2,4,24,64]{3,2,1,0:T(8,128)S(1)} %fusion.70) | data formatting | bytes 98304 | tf_op jit(solution)/shard_map/reshape | solution.py:60
  341.5 3.9 collective-permute-start.47
  351.1 3.9 collective-permute-start.49
  388.0 4.0 %collective-permute-done.55 = f32[2,1,48,128]{2,1,3,0:T(1,128)S(1)} collective-permute-done((f32[2,1,48,128]{2,1,3,0:T(1,128)S(1)}, f32[2,1,48,128]{2,1,3,0:T(1,128)S(1)}, u32[]{:S(2)}, u32[]{:S(2)}) %collective-permute-start.55) | collective-permute-done | bytes 49184 | tf_op jit(solution)/shard_map/ppermute | solution.py:23
  (323 shorter events, 198.1 us)
Async XLA Ops:
  0.0 29.7 %collective-permute-start = (f32[1,8,48,128]{3,2,1,0:T(8,128)}, f32[1,8,48,128]{3,2,1,0:T(8,128)S(1)}, u32[]{:S(2)}, u32[]{:S(2)}) collective-permute-start(f32[1,8,48,128]{3,2,1,0:T(8,128)} %param.2), channel_id=1, source_target_pairs={{0,16},{16,32},{32,48},{48,64},{64,80},{80,96},{96,112},{112,128},... | collective-permute-start | bytes 589832 | tf_op jit(solution)/shard_map/ppermute | solution.py:34
  0.0 31.6 %collective-permute-start.1 = (f32[1,8,48,128]{3,2,1,0:T(8,128)}, f32[1,8,48,128]{3,2,1,0:T(8,128)S(1)}, u32[]{:S(2)}, u32[]{:S(2)}) collective-permute-start(f32[1,8,48,128]{3,2,1,0:T(8,128)} %param.2), channel_id=1, source_target_pairs={{0,240},{16,0},{32,16},{48,32},{64,48},{80,64},{96,80},{112,96},{1... | collective-permute-start | bytes 589832 | tf_op jit(solution)/shard_map/ppermute | solution.py:34
  5.4 33.3 %collective-permute-start.2 = (f32[2,1,48,128]{2,1,3,0:T(1,128)S(1)}, f32[2,1,48,128]{2,1,3,0:T(1,128)S(1)}, u32[]{:S(2)}, u32[]{:S(2)}) collective-permute-start(f32[2,1,48,128]{2,1,3,0:T(1,128)S(1)} %broadcast.246), channel_id=1, source_target_pairs={{1,0},{2,1},{3,2},{4,3},{5,4},{6,5},{7,6},{8,7},{9,8},{10,9},{11,1... | collective-permute-start | bytes 147464 | tf_op jit(solution)/shard_map/ppermute | solution.py:25
  10.2 28.5 %collective-permute-start.3 = (f32[2,1,48,128]{2,1,3,0:T(1,128)S(1)}, f32[2,1,48,128]{2,1,3,0:T(1,128)S(1)}, u32[]{:S(2)}, u32[]{:S(2)}) collective-permute-start(f32[2,1,48,128]{2,1,3,0:T(1,128)S(1)} %broadcast.246), channel_id=1, source_target_pairs={{0,1},{1,2},{2,3},{3,4},{4,5},{5,6},{6,7},{7,8},{8,9},{9,10},{10,1... | collective-permute-start | bytes 147464 | tf_op jit(solution)/shard_map/ppermute | solution.py:23
  21.8 82.0 %collective-permute-start.6 = (f32[2,1,24,64]{3,2,1,0:T(8,128)}, f32[2,1,24,64]{3,2,1,0:T(8,128)}, u32[]{:S(2)}, u32[]{:S(2)}) collective-permute-start(f32[2,1,24,64]{3,2,1,0:T(8,128)} %broadcast.249), channel_id=1, source_target_pairs={{1,0},{2,1},{3,2},{4,3},{5,4},{6,5},{7,6},{8,7},{9,8},{10,9},{11,1... | collective-permute-start | bytes 36872 | tf_op jit(solution)/shard_map/ppermute | solution.py:25
  29.7 74.1 %collective-permute-start.7 = (f32[2,1,24,64]{3,2,1,0:T(8,128)}, f32[2,1,24,64]{3,2,1,0:T(8,128)}, u32[]{:S(2)}, u32[]{:S(2)}) collective-permute-start(f32[2,1,24,64]{3,2,1,0:T(8,128)} %broadcast.249), channel_id=1, source_target_pairs={{0,1},{1,2},{2,3},{3,4},{4,5},{5,6},{6,7},{7,8},{8,9},{9,10},{10,1... | collective-permute-start | bytes 36872 | tf_op jit(solution)/shard_map/ppermute | solution.py:23
  32.2 89.8 %collective-permute-start.10 = (f32[2,1,12,32]{3,2,1,0:T(8,128)}, f32[2,1,12,32]{3,2,1,0:T(8,128)}, u32[]{:S(2)}, u32[]{:S(2)}) collective-permute-start(f32[2,1,12,32]{3,2,1,0:T(8,128)} %broadcast.253), channel_id=1, source_target_pairs={{1,0},{2,1},{3,2},{4,3},{5,4},{6,5},{7,6},{8,7},{9,8},{10,9},{11,1... | collective-permute-start | bytes 9224 | tf_op jit(solution)/shard_map/ppermute | solution.py:25
  47.7 9.5 %collective-permute-start.5 = (f32[2,1,48,128]{2,1,3,0:T(1,128)}, f32[2,1,48,128]{2,1,3,0:T(1,128)}, u32[]{:S(2)}, u32[]{:S(2)}) collective-permute-start(f32[2,1,48,128]{2,1,3,0:T(1,128)} %get-tuple-element.62), channel_id=1, source_target_pairs={{0,1},{1,2},{2,3},{3,4},{4,5},{5,6},{6,7},{7,8},{8,9},{9,10},{10,1... | collective-permute-start | bytes 147464 | tf_op jit(solution)/shard_map/ppermute | solution.py:23
  53.0 69.0 %collective-permute-start.11 = (f32[2,1,12,32]{3,2,1,0:T(8,128)}, f32[2,1,12,32]{3,2,1,0:T(8,128)S(1)}, u32[]{:S(2)}, u32[]{:S(2)}) collective-permute-start(f32[2,1,12,32]{3,2,1,0:T(8,128)} %broadcast.253), channel_id=1, source_target_pairs={{0,1},{1,2},{2,3},{3,4},{4,5},{5,6},{6,7},{7,8},{8,9},{9,10},{10,1... | collective-permute-start | bytes 9224 | tf_op jit(solution)/shard_map/ppermute | solution.py:23
  57.2 78.1 %collective-permute-start.14 = (f32[2,1,6,16]{3,0,2,1:T(2,128)S(1)}, f32[2,1,6,16]{3,0,2,1:T(2,128)S(1)}, u32[]{:S(2)}, u32[]{:S(2)}) collective-permute-start(f32[2,1,6,16]{3,0,2,1:T(2,128)S(1)} %broadcast.256), channel_id=1, source_target_pairs={{1,0},{2,1},{3,2},{4,3},{5,4},{6,5},{7,6},{8,7},{9,8},{10,9},{11,1... | collective-permute-start | bytes 2312 | tf_op jit(solution)/shard_map/ppermute | solution.py:25
  106.8 7.8 %collective-permute-start.9 = (f32[2,1,24,64]{3,2,1,0:T(8,128)S(1)}, f32[2,1,24,64]{3,2,1,0:T(8,128)S(1)}, u32[]{:S(2)}, u32[]{:S(2)}) collective-permute-start(f32[2,1,24,64]{3,2,1,0:T(8,128)S(1)} %get-tuple-element.102), channel_id=1, source_target_pairs={{0,1},{1,2},{2,3},{3,4},{4,5},{5,6},{6,7},{7,8},{8,9},{9,10},{10,1... | collective-permute-start | bytes 36872 | tf_op jit(solution)/shard_map/ppermute | solution.py:23
  110.8 24.5 %collective-permute-start.15 = (f32[2,1,6,16]{3,0,2,1:T(2,128)S(1)}, f32[2,1,6,16]{3,0,2,1:T(2,128)S(1)}, u32[]{:S(2)}, u32[]{:S(2)}) collective-permute-start(f32[2,1,6,16]{3,0,2,1:T(2,128)S(1)} %broadcast.256), channel_id=1, source_target_pairs={{0,1},{1,2},{2,3},{3,4},{4,5},{5,6},{6,7},{7,8},{8,9},{9,10},{10,1... | collective-permute-start | bytes 2312 | tf_op jit(solution)/shard_map/ppermute | solution.py:23
  127.1 7.7 %collective-permute-start.13 = (f32[2,1,12,32]{3,2,1,0:T(8,128)S(1)}, f32[2,1,12,32]{3,2,1,0:T(8,128)S(1)}, u32[]{:S(2)}, u32[]{:S(2)}) collective-permute-start(f32[2,1,12,32]{3,2,1,0:T(8,128)S(1)} %get-tuple-element.142), channel_id=1, source_target_pairs={{0,1},{1,2},{2,3},{3,4},{4,5},{5,6},{6,7},{7,8},{8,9},{9,10},{10,1... | collective-permute-start | bytes 9224 | tf_op jit(solution)/shard_map/ppermute | solution.py:23
  137.3 7.6 %collective-permute-start.17 = (f32[2,1,6,16]{3,0,2,1:T(2,128)S(1)}, f32[2,1,6,16]{3,0,2,1:T(2,128)S(1)}, u32[]{:S(2)}, u32[]{:S(2)}) collective-permute-start(f32[2,1,6,16]{3,0,2,1:T(2,128)S(1)} %get-tuple-element.5), channel_id=1, source_target_pairs={{0,1},{1,2},{2,3},{3,4},{4,5},{5,6},{6,7},{7,8},{8,9},{9,10},{10,1... | collective-permute-start | bytes 2312 | tf_op jit(solution)/shard_map/ppermute | solution.py:23
  147.0 7.6 %collective-permute-start.19 = (f32[2,1,6,16]{3,0,2,1:T(2,128)S(1)}, f32[2,1,6,16]{3,0,2,1:T(2,128)S(1)}, u32[]{:S(2)}, u32[]{:S(2)}) collective-permute-start(f32[2,1,6,16]{3,0,2,1:T(2,128)S(1)} %fusion.178), channel_id=1, source_target_pairs={{0,1},{1,2},{2,3},{3,4},{4,5},{5,6},{6,7},{7,8},{8,9},{9,10},{10,1... | collective-permute-start | bytes 2312 | tf_op jit(solution)/shard_map/ppermute | solution.py:23
  156.6 7.6 %collective-permute-start.21 = (f32[2,1,6,16]{3,0,2,1:T(2,128)S(1)}, f32[2,1,6,16]{3,0,2,1:T(2,128)S(1)}, u32[]{:S(2)}, u32[]{:S(2)}) collective-permute-start(f32[2,1,6,16]{3,0,2,1:T(2,128)S(1)} %fusion.180), channel_id=1, source_target_pairs={{0,1},{1,2},{2,3},{3,4},{4,5},{5,6},{6,7},{7,8},{8,9},{9,10},{10,1... | collective-permute-start | bytes 2312 | tf_op jit(solution)/shard_map/ppermute | solution.py:23
  166.3 7.6 %collective-permute-start.23 = (f32[2,1,6,16]{3,0,2,1:T(2,128)S(1)}, f32[2,1,6,16]{3,0,2,1:T(2,128)S(1)}, u32[]{:S(2)}, u32[]{:S(2)}) collective-permute-start(f32[2,1,6,16]{3,0,2,1:T(2,128)S(1)} %fusion.182), channel_id=1, source_target_pairs={{0,1},{1,2},{2,3},{3,4},{4,5},{5,6},{6,7},{7,8},{8,9},{9,10},{10,1... | collective-permute-start | bytes 2312 | tf_op jit(solution)/shard_map/ppermute | solution.py:23
  175.9 7.6 %collective-permute-start.25 = (f32[2,1,6,16]{3,0,2,1:T(2,128)S(1)}, f32[2,1,6,16]{3,0,2,1:T(2,128)S(1)}, u32[]{:S(2)}, u32[]{:S(2)}) collective-permute-start(f32[2,1,6,16]{3,0,2,1:T(2,128)S(1)} %fusion.184), channel_id=1, source_target_pairs={{0,1},{1,2},{2,3},{3,4},{4,5},{5,6},{6,7},{7,8},{8,9},{9,10},{10,1... | collective-permute-start | bytes 2312 | tf_op jit(solution)/shard_map/ppermute | solution.py:23
  186.0 7.7 %collective-permute-start.27 = (f32[2,1,12,32]{3,2,1,0:T(8,128)S(1)}, f32[2,1,12,32]{3,2,1,0:T(8,128)S(1)}, u32[]{:S(2)}, u32[]{:S(2)}) collective-permute-start(f32[2,1,12,32]{3,2,1,0:T(8,128)S(1)} %get-tuple-element.132), channel_id=1, source_target_pairs={{0,1},{1,2},{2,3},{3,4},{4,5},{5,6},{6,7},{7,8},{8,9},{9,10},{10,1... | collective-permute-start | bytes 9224 | tf_op jit(solution)/shard_map/ppermute | solution.py:23
  196.5 7.8 %collective-permute-start.29 = (f32[2,1,24,64]{3,2,1,0:T(8,128)S(1)}, f32[2,1,24,64]{3,2,1,0:T(8,128)S(1)}, u32[]{:S(2)}, u32[]{:S(2)}) collective-permute-start(f32[2,1,24,64]{3,2,1,0:T(8,128)S(1)} %get-tuple-element.92), channel_id=1, source_target_pairs={{0,1},{1,2},{2,3},{3,4},{4,5},{5,6},{6,7},{7,8},{8,9},{9,10},{10,1... | collective-permute-start | bytes 36872 | tf_op jit(solution)/shard_map/ppermute | solution.py:23
  208.0 9.0 %collective-permute-start.31 = (f32[2,1,48,128]{2,1,3,0:T(1,128)S(1)}, f32[2,1,48,128]{2,1,3,0:T(1,128)S(1)}, u32[]{:S(2)}, u32[]{:S(2)}) collective-permute-start(f32[2,1,48,128]{2,1,3,0:T(1,128)S(1)} %get-tuple-element.52), channel_id=1, source_target_pairs={{0,1},{1,2},{2,3},{3,4},{4,5},{5,6},{6,7},{7,8},{8,9},{9,10},{10,1... | collective-permute-start | bytes 147464 | tf_op jit(solution)/shard_map/ppermute | solution.py:23
  221.2 9.0 %collective-permute-start.33 = (f32[2,1,48,128]{2,1,3,0:T(1,128)S(1)}, f32[2,1,48,128]{2,1,3,0:T(1,128)S(1)}, u32[]{:S(2)}, u32[]{:S(2)}) collective-permute-start(f32[2,1,48,128]{2,1,3,0:T(1,128)S(1)} %get-tuple-element.42), channel_id=1, source_target_pairs={{0,1},{1,2},{2,3},{3,4},{4,5},{5,6},{6,7},{7,8},{8,9},{9,10},{10,1... | collective-permute-start | bytes 147464 | tf_op jit(solution)/shard_map/ppermute | solution.py:23
  234.3 9.0 %collective-permute-start.35 = (f32[2,1,48,128]{2,1,3,0:T(1,128)S(1)}, f32[2,1,48,128]{2,1,3,0:T(1,128)S(1)}, u32[]{:S(2)}, u32[]{:S(2)}) collective-permute-start(f32[2,1,48,128]{2,1,3,0:T(1,128)S(1)} %get-tuple-element.32), channel_id=1, source_target_pairs={{0,1},{1,2},{2,3},{3,4},{4,5},{5,6},{6,7},{7,8},{8,9},{9,10},{10,1... | collective-permute-start | bytes 147464 | tf_op jit(solution)/shard_map/ppermute | solution.py:23
  285.2 7.8 %collective-permute-start.37 = (f32[2,1,24,64]{3,2,1,0:T(8,128)S(1)}, f32[2,1,24,64]{3,2,1,0:T(8,128)S(1)}, u32[]{:S(2)}, u32[]{:S(2)}) collective-permute-start(f32[2,1,24,64]{3,2,1,0:T(8,128)S(1)} %get-tuple-element.82), channel_id=1, source_target_pairs={{0,1},{1,2},{2,3},{3,4},{4,5},{5,6},{6,7},{7,8},{8,9},{9,10},{10,1... | collective-permute-start | bytes 36872 | tf_op jit(solution)/shard_map/ppermute | solution.py:23
  302.5 7.7 %collective-permute-start.39 = (f32[2,1,12,32]{3,2,1,0:T(8,128)S(1)}, f32[2,1,12,32]{3,2,1,0:T(8,128)S(1)}, u32[]{:S(2)}, u32[]{:S(2)}) collective-permute-start(f32[2,1,12,32]{3,2,1,0:T(8,128)S(1)} %get-tuple-element.122), channel_id=1, source_target_pairs={{0,1},{1,2},{2,3},{3,4},{4,5},{5,6},{6,7},{7,8},{8,9},{9,10},{10,1... | collective-permute-start | bytes 9224 | tf_op jit(solution)/shard_map/ppermute | solution.py:23
  322.2 7.6 %collective-permute-start.43 = (f32[2,1,6,16]{3,0,2,1:T(2,128)S(1)}, f32[2,1,6,16]{3,0,2,1:T(2,128)S(1)}, u32[]{:S(2)}, u32[]{:S(2)}) collective-permute-start(f32[2,1,6,16]{3,0,2,1:T(2,128)S(1)} %fusion.167), channel_id=1, source_target_pairs={{0,1},{1,2},{2,3},{3,4},{4,5},{5,6},{6,7},{7,8},{8,9},{9,10},{10,1... | collective-permute-start | bytes 2312 | tf_op jit(solution)/shard_map/ppermute | solution.py:23
  331.8 7.6 %collective-permute-start.45 = (f32[2,1,6,16]{3,0,2,1:T(2,128)S(1)}, f32[2,1,6,16]{3,0,2,1:T(2,128)S(1)}, u32[]{:S(2)}, u32[]{:S(2)}) collective-permute-start(f32[2,1,6,16]{3,0,2,1:T(2,128)S(1)} %fusion.169), channel_id=1, source_target_pairs={{0,1},{1,2},{2,3},{3,4},{4,5},{5,6},{6,7},{7,8},{8,9},{9,10},{10,1... | collective-permute-start | bytes 2312 | tf_op jit(solution)/shard_map/ppermute | solution.py:23
  341.5 7.6 %collective-permute-start.47 = (f32[2,1,6,16]{3,0,2,1:T(2,128)S(1)}, f32[2,1,6,16]{3,0,2,1:T(2,128)S(1)}, u32[]{:S(2)}, u32[]{:S(2)}) collective-permute-start(f32[2,1,6,16]{3,0,2,1:T(2,128)S(1)} %fusion.171), channel_id=1, source_target_pairs={{0,1},{1,2},{2,3},{3,4},{4,5},{5,6},{6,7},{7,8},{8,9},{9,10},{10,1... | collective-permute-start | bytes 2312 | tf_op jit(solution)/shard_map/ppermute | solution.py:23
  351.1 7.6 %collective-permute-start.49 = (f32[2,1,6,16]{3,0,2,1:T(2,128)S(1)}, f32[2,1,6,16]{3,0,2,1:T(2,128)S(1)}, u32[]{:S(2)}, u32[]{:S(2)}) collective-permute-start(f32[2,1,6,16]{3,0,2,1:T(2,128)S(1)} %fusion.173), channel_id=1, source_target_pairs={{0,1},{1,2},{2,3},{3,4},{4,5},{5,6},{6,7},{7,8},{8,9},{9,10},{10,1... | collective-permute-start | bytes 2312 | tf_op jit(solution)/shard_map/ppermute | solution.py:23
  361.2 7.7 %collective-permute-start.51 = (f32[2,1,12,32]{3,2,1,0:T(8,128)S(1)}, f32[2,1,12,32]{3,2,1,0:T(8,128)S(1)}, u32[]{:S(2)}, u32[]{:S(2)}) collective-permute-start(f32[2,1,12,32]{3,2,1,0:T(8,128)S(1)} %get-tuple-element.112), channel_id=1, source_target_pairs={{0,1},{1,2},{2,3},{3,4},{4,5},{5,6},{6,7},{7,8},{8,9},{9,10},{10,1... | collective-permute-start | bytes 9224 | tf_op jit(solution)/shard_map/ppermute | solution.py:23
  371.6 7.8 %collective-permute-start.53 = (f32[2,1,24,64]{3,2,1,0:T(8,128)S(1)}, f32[2,1,24,64]{3,2,1,0:T(8,128)S(1)}, u32[]{:S(2)}, u32[]{:S(2)}) collective-permute-start(f32[2,1,24,64]{3,2,1,0:T(8,128)S(1)} %get-tuple-element.72), channel_id=1, source_target_pairs={{0,1},{1,2},{2,3},{3,4},{4,5},{5,6},{6,7},{7,8},{8,9},{9,10},{10,1... | collective-permute-start | bytes 36872 | tf_op jit(solution)/shard_map/ppermute | solution.py:23
  383.1 9.0 %collective-permute-start.55 = (f32[2,1,48,128]{2,1,3,0:T(1,128)S(1)}, f32[2,1,48,128]{2,1,3,0:T(1,128)S(1)}, u32[]{:S(2)}, u32[]{:S(2)}) collective-permute-start(f32[2,1,48,128]{2,1,3,0:T(1,128)S(1)} %get-tuple-element.22), channel_id=1, source_target_pairs={{0,1},{1,2},{2,3},{3,4},{4,5},{5,6},{6,7},{7,8},{8,9},{9,10},{10,1... | collective-permute-start | bytes 147464 | tf_op jit(solution)/shard_map/ppermute | solution.py:23
  (39 other events, 305.5 us)
where the time goes:
time: 396 us; the launch traced here: 394 us
  starting transfers between devices  172 us (43%)
  waiting for transfers between devices  89.5 us (23%)
  local copies, waits for them, and re-layouts  89.4 us (23%)
  other arithmetic  42 us (11%)
    ppermute x27, starting transfers between devices, with_halo(): lax.ppermute(tail, axis, [(i, (i + 1) % count) for i in range(ends)])  96.4 us
    ppermute x27, waiting for transfers between devices, with_halo(): lax.ppermute(tail, axis, [(i, (i + 1) % count) for i in range(ends)])  84 us
    ppermute x27, starting transfers between devices, with_halo(): lax.ppermute(head, axis, [((i + 1) % count, i) for i in range(ends)])  67.2 us
    reshape x4, local copies, waits for them, and re-layouts, restrict(): values.reshape(shape[0], shape[1] // 2, 2, shape[2] // 2, 2, shape[3] //...  63 us
    reduce_sum x8, other arithmetic, restrict(): return jnp.sum(grouped, axis=(2, 4, 6)) * 0.125  23.7 us
    ppermute x4, starting transfers between devices, shifted(): lax.ppermute(shard, axis, [(i, (i + by) % peers) for i in range(peers)])  8.26 us
  transfers between devices with their start and end apart: 58, of which 28 were waited for; matrix products, arithmetic and copies ran while one was open for 18% of the time, Pallas kernels for 0%

commit v1 on v0

v1 whole, which is shorter than its diff:
```python
import functools

import jax
import jax.numpy as jnp
from jax import lax
from jax.experimental import pallas as pl
from jax.experimental.pallas import tpu as pltpu
from jax.sharding import PartitionSpec as P

MESH = pl.DeviceIdType.MESH

NZ, NY, NX = 128, 48, 128
SWEEPS = 6
screening = 0.001
relaxation = 0.8

STEP = [0.25**level for level in range(4)]
CENTRE = [6.0 * step + screening for step in STEP]
KEEP = 1.0 - relaxation
PULL = [relaxation / centre for centre in CENTRE]
SIDE = [pull * step for pull, step in zip(PULL, STEP)]

ROWS1 = 48
MSG = 16


def turn(value, by, axis):
    return pltpu.roll(value, by % value.shape[axis], axis)


def lanes(rows):
    return lax.broadcasted_iota(jnp.int32, (rows, 128), 1)


def in_plane(value, lane_step):
    return (turn(value, 1, 0) + turn(value, -1, 0)) + (turn(value, lane_step, 1) + turn(value, -lane_step, 1))


def swapped(value, bit):
    first = (lanes(value.shape[0]) & bit) == 0
    return jnp.where(first, turn(value, -bit, 1), turn(value, bit, 1))


def total(parts):
    parts = [part for part in parts if part is not None]
    while len(parts) > 1:
        parts = [a + b for a, b in zip(parts[::2], parts[1::2])] + parts[len(parts) // 2 * 2 :]
    return parts[0] if parts else None


def kernel(
    n_orb, n_slab,
    occ_ref, orb_ref, out_ref,
    own, right, occ_out, occ_in, f, v2, v, v1, pe1, f1, src1, e1, pe2, f1_out, f1_in, gather, e2,
    ret_out, ret_in,
    local_sem, orb_send, orb_recv, occ_sems, gat_send, gat_recv, f1_send, f1_recv, f_send, f_recv, ret_send, ret_recv,
):
    o, s = lax.axis_index("orb"), lax.axis_index("slab")
    right_orb, left_orb = lax.rem(o + 1, n_orb), lax.rem(o + n_orb - 1, n_orb)
    above, below = lax.rem(s + 1, n_slab), lax.rem(s + n_slab - 1, n_slab)
    odd = lax.rem(s, 2)

    def at_slab(index):
        return {"slab": index}

    def at_orb(index):
        return {"orb": index}

    mine = pltpu.make_async_copy(orb_ref.at[0], own, local_sem)
    mine.start()

    barrier = pltpu.get_barrier_semaphore()
    pl.semaphore_signal(barrier, inc=1, device_id=at_orb(left_orb), device_id_type=MESH)
    pl.semaphore_signal(barrier, inc=1, device_id=at_orb(right_orb), device_id_type=MESH)
    for k in range(1, n_slab):
        pl.semaphore_signal(barrier, inc=1, device_id=at_slab(lax.rem(s + k, n_slab)), device_id_type=MESH)

    occ_out[...] = jnp.full((8, 128), occ_ref[0], jnp.float32)
    for g in range(2):
        for slot in (0, 17):
            gather[pl.ds((g * 18 + slot) * MSG, MSG), :] = jnp.zeros((MSG, 128), jnp.float32)
    e2[...] = jnp.zeros_like(e2)
    src1[...] = jnp.zeros_like(src1)
    low = jnp.where(s > 0, 1.0, 0.0).astype(jnp.float32)
    high = jnp.where(s < n_slab - 1, 1.0, 0.0).astype(jnp.float32)

    def inside(plane, count):
        return low if plane < 0 else high if plane >= count else 1.0

    pl.semaphore_wait(barrier, n_slab + 1)

    halves = []
    for h in range(2):
        planes = pl.ds(4 * h, 4)
        halves.append(pltpu.make_async_remote_copy(
            orb_ref.at[0, planes], right.at[planes], orb_send.at[h], orb_recv.at[h],
            device_id=at_orb(left_orb), device_id_type=MESH))
        halves[-1].start()
    occ_copy = pltpu.make_async_remote_copy(
        occ_out, occ_in, occ_sems.at[0], occ_sems.at[1], device_id=at_orb(left_orb), device_id_type=MESH)
    occ_copy.start()

    mine.wait()
    for h in range(2):
        halves[h].wait_recv()
        for p in range(4 * h, 4 * h + 4):
            f[3 + p] = own[p] * right[p]

    pending = []

    def send(src, dst, send_sem, recv_sem, device):
        copy = pltpu.make_async_remote_copy(src, dst, send_sem, recv_sem, device_id=device, device_id_type=MESH)
        copy.start()
        pending.append(copy)
        return copy

    def restricted(pair, beyond, source, centre, side, bit):
        beyond = total([part for plane in beyond for part in plane[:2]])
        terms = []
        if pair:
            even, odd_, before, after = [total([plane[i] for plane in pair]) for i in range(4)]
            both = even + odd_
            terms.append(centre * both)
            around = total([both + both, before, after, turn(both, bit, 1), turn(both, -bit, 1), beyond])
        else:
            around = beyond
        terms.append(side * around)
        terms += [part for plane in source for part in plane]
        mean = total(terms)
        return 0.125 * (mean + swapped(mean, bit))

    def fine_rows(ref, plane):
        even, odd_ = ref[plane, pl.ds(0, 24, stride=2), :], ref[plane, pl.ds(1, 24, stride=2), :]
        return even, odd_, turn(odd_, 1, 0), turn(even, -1, 0)

    def put_src1(slot, value):
        src1[slot, 8:32, :] = value
        src1[slot, 7:8, :] = value[23:24]
        src1[slot, 32:33, :] = value[0:1]

    def coarse_rows(slot):
        return [src1[slot, pl.ds(8 + start, MSG, stride=2), :] for start in (0, 1, -1, 2)]

    lane16 = lanes(MSG)
    place16 = (lane16 + 2 * odd) & 3

    def send_level2(g, have):
        parts = {}
        for d in range(-1, 3):
            pair = [coarse_rows(q + 1) for q in (2 * d, 2 * d + 1) if q in have]
            beyond = [coarse_rows(q + 1) for q in (2 * d - 1, 2 * d + 2) if q in have]
            parts[d] = restricted(pair, beyond, [], KEEP, SIDE[1], 2)
        packed = jnp.where(place16 == 0, parts[0], jnp.where(place16 == 1, parts[1], jnp.where(place16 == 2, parts[2], parts[-1])))
        base = g * 18 * MSG
        slot = pl.ds(pl.multiple_of(base + (s + 1) * MSG, MSG), MSG)
        gather[slot, :] = packed
        for k in range(1, n_slab):
            pltpu.make_async_remote_copy(
                gather.at[slot], gather.at[slot], gat_send.at[g], gat_recv.at[g],
                device_id=at_slab(lax.rem(s + k, n_slab)), device_id_type=MESH).start()

    def gathered(g):
        most = gather.at[pl.ds(g * 18 * MSG, (n_slab - 1) * MSG)]
        return pltpu.make_async_remote_copy(
            most, most, gat_send.at[g], gat_recv.at[g], device_id=at_slab(above), device_id_type=MESH)

    row8 = lax.broadcasted_iota(jnp.int32, (8, 128), 0)
    lane8 = lanes(8)
    first_row, last_row = row8 == 0, row8 == 7

    def level2_sides(u):
        result = []
        for y in range(12):
            here = u[y]
            up = jnp.where(last_row, 0.0, turn(turn(here, 3, 1), -1, 0))
            down = jnp.where(first_row, 0.0, turn(turn(here, -3, 1), 1, 0))
            up = jnp.where((lane8 & 3) == 3, up, turn(here, -1, 1))
            down = jnp.where((lane8 & 3) == 0, down, turn(here, 1, 1))
            x = turn(here, 4, 1) + turn(here, -4, 1)
            result.append(total([u[(y + 1) % 12], u[(y + 11) % 12], up, down, x]))
        return result

    def level3_sides(u):
        result = []
        lower = (lane8 & 2) == 0
        for y in range(6):
            here = u[y]
            a, b = turn(here, -2, 1), turn(here, 2, 1)
            far = jnp.where(lower, jnp.where(first_row, 0.0, turn(a, 1, 0)), jnp.where(last_row, 0.0, turn(b, -1, 0)))
            x = turn(here, 8, 1) + turn(here, -8, 1)
            result.append(total([u[(y + 1) % 6], u[(y + 5) % 6], jnp.where(lower, a, b), far, x]))
        return result

    def solve_level2(g):
        base = g * 18 * MSG + MSG
        source = []
        for y in range(12):
            at = [gather[pl.ds(base + y + MSG * k, 8, stride=2 * MSG), :] for k in (0, 1)]
            after = gather[pl.ds(base + y + MSG * 2, 8, stride=2 * MSG), :]
            before = gather[pl.ds(base + y - MSG, 8, stride=2 * MSG), :]
            source.append(jnp.where((lane8 & 3) == 3, after, at[0]) + jnp.where((lane8 & 3) == 0, before, at[1]))
        sides = level2_sides(source)
        residual = [KEEP * a + SIDE[2] * b for a, b in zip(source, sides)]
        source3 = []
        for y in range(6):
            pair = residual[2 * y] + residual[2 * y + 1]
            pair = pair + swapped(pair, 1)
            source3.append(0.125 * (pair + swapped(pair, 4)))
        pull = [PULL[3] * a for a in source3]
        iterate = pull
        for _ in range(SWEEPS - 1):
            sides = level3_sides(iterate)
            iterate = [KEEP * a + b + SIDE[3] * c for a, b, c in zip(iterate, pull, sides)]
        pull = [PULL[2] * a for a in source]
        u = [a + iterate[y // 2] for y, a in enumerate(pull)]
        sides = level2_sides(u)
        for y in range(12):
            e2[24 * y + 8 : 24 * y + 16, :] = KEEP * u[y] + pull[y] + SIDE[2] * sides[y]

    def spread_level2(ds):
        row = (s + 1) // 2 - 1
        a = e2[pl.ds(8 + row, MSG, stride=24), :]
        b = e2[pl.ds(9 + row, MSG, stride=24), :]
        middle = jnp.where(odd == 1, a, b)
        for d in ds:
            value = jnp.where(place16 == d % 4, a if d < 0 else middle if d < 2 else b, 0.0)
            value = value + swapped(value, 1)
            value = value + swapped(value, 2)
            pe2[d + 2, pl.ds(0, MSG, stride=2), :] = value
            pe2[d + 2, pl.ds(1, MSG, stride=2), :] = value

    even24 = (lanes(24) & 1) == 0

    def packed(a, b):
        return jnp.where(even24, a, b)

    def unpacked(value):
        return jnp.where(even24, value, turn(value, 1, 1)), jnp.where(even24, turn(value, -1, 1), value)

    def correct_level1(reach):
        u = {}
        for q in range(-reach - 1, 5 + reach):
            u[q] = PULL[1] * f1[q + 3] + pe2[q // 2 + 2, 0:24, :]
        for q in range(-reach, 4 + reach):
            sides = total([u[q - 1], u[q + 1], in_plane(u[q], 2)])
            value = KEEP * u[q] + PULL[1] * f1[q + 3] + (SIDE[1] * inside(q, 4)) * sides
            pe1[q + 2, pl.ds(0, 24, stride=2), :] = value
            pe1[q + 2, pl.ds(1, 24, stride=2), :] = value

    for q in range(-1, 5):
        pair = [fine_rows(f, p + 3) for p in (2 * q, 2 * q + 1) if 0 <= p < 8]
        beyond = [fine_rows(f, p + 3) for p in (2 * q - 1, 2 * q + 2) if 0 <= p < 8]
        part = restricted(pair, beyond, [], KEEP, SIDE[0] * inside(q, 4), 1)
        put_src1(q + 1, part)
    send_level2(0, range(-1, 5))
    parts = [src1[q + 1, 8:32, :] for q in range(-1, 5)]
    for i in range(2):
        f1_out[0, i] = packed(parts[2 * i], parts[2 * i + 1])
        f1_out[1, i] = packed(parts[2 * i + 2], parts[2 * i + 3])
    for side, device in ((0, below), (1, above)):
        send(f1_out.at[side, pl.ds(0, 2)], f1_in.at[side, pl.ds(0, 2)], f1_send.at[side], f1_recv.at[side], at_slab(device))
    send(f.at[pl.ds(3, 3)], f.at[pl.ds(11, 3)], f_send.at[0], f_recv.at[0], at_slab(below))
    send(f.at[pl.ds(8, 3)], f.at[pl.ds(0, 3)], f_send.at[1], f_recv.at[1], at_slab(above))

    gathered(0).wait_recv()
    solve_level2(0)
    spread_level2(range(-2, 4))
    pending[0].wait_recv()
    pending[1].wait_recv()
    under = [low * plane for i in range(2) for plane in unpacked(f1_in[1, i])]
    over = [high * plane for i in range(2) for plane in unpacked(f1_in[0, i])]
    f1[0] = under[0]
    f1[1] = under[1]
    f1[2] = under[2] + parts[0]
    f1[3] = under[3] + parts[1]
    f1[4] = parts[2]
    f1[5] = parts[3]
    f1[6] = parts[4] + over[0]
    f1[7] = parts[5] + over[1]
    f1[8] = over[2]
    f1[9] = over[3]
    correct_level1(2)
    pending[2].wait_recv()
    pending[3].wait_recv()
    for p in range(-3, 11):
        v2[p + 3] = (PULL[0] * inside(p, 8)) * f[p + 3] + pe1[p // 2 + 2]

    def smooth(ref, slot, plane):
        here = ref[slot]
        sides = total([ref[slot - 1], ref[slot + 1], in_plane(here, 1)])
        flag = inside(plane, 8)
        return KEEP * here + (PULL[0] * flag) * f[plane + 3] + (SIDE[0] * flag) * sides

    for p in range(-2, 10):
        v[p + 2] = smooth(v2, p + 3, p)

    for p in range(-1, 9):
        v1[p + 1] = smooth(v, p + 2, p)
    for q in range(4):
        pair = [fine_rows(v1, p + 1) for p in (2 * q, 2 * q + 1)]
        beyond = [fine_rows(v1, p + 1) for p in (2 * q - 1, 2 * q + 2)]
        source = [fine_rows(f, p + 3)[:2] for p in (2 * q, 2 * q + 1)]
        put_src1(q + 1, restricted(pair, beyond, source, -CENTRE[0], STEP[0], 1))
    send_level2(1, range(4))
    parts = [src1[q + 1, 8:32, :] for q in range(4)]
    for side, device in ((0, below), (1, above)):
        f1_out[side, 2] = packed(parts[2 * side], parts[2 * side + 1])
        send(f1_out.at[side, pl.ds(2, 1)], f1_in.at[side, pl.ds(2, 1)], f1_send.at[side + 2], f1_recv.at[side + 2], at_slab(device))
    for q in range(4):
        f1[q + 3] = parts[q]
    gathered(1).wait_recv()
    solve_level2(1)
    spread_level2(range(-1, 3))
    pending[4].wait_recv()
    pending[5].wait_recv()
    under, over = unpacked(f1_in[1, 2]), unpacked(f1_in[0, 2])
    for i in range(2):
        f1[1 + i] = low * under[i]
        f1[7 + i] = high * over[i]
    correct_level1(1)
    for p in range(-1, 9):
        v2[p + 3] = v1[p + 1] + pe1[p // 2 + 2]

    occ_copy.wait_recv()
    mine_occ, right_occ = -occ_out[0:1, :], -occ_in[0:1, :]
    for h in range(4):
        for p in range(2 * h, 2 * h + 2):
            potential = smooth(v2, p + 3, p)
            ret_out[p] = (potential * mine_occ) * own[p]
            v[p] = (potential * right_occ) * right[p]
        planes = pl.ds(2 * h, 2)
        send(ret_out.at[planes], ret_in.at[planes], ret_send.at[h], ret_recv.at[h], at_orb(right_orb))
    for h in range(4):
        pending[6 + h].wait_recv()
        for p in range(2 * h, 2 * h + 2):
            out_ref[0, p] = v[p] + ret_in[p]

    for copy in halves:
        copy.wait_send()
    occ_copy.wait_send()
    for copy in pending:
        copy.wait_send()
    for g in range(2):
        gathered(g).wait_send()


def on_device(n_orb, n_slab, orbitals, occupations):
    vmem, dma = pltpu.VMEM, pltpu.SemaphoreType.DMA
    f32 = jnp.float32

    def fine(planes):
        return vmem((planes, NY, NX), f32)

    return pl.pallas_call(
        functools.partial(kernel, n_orb, n_slab),
        out_shape=jax.ShapeDtypeStruct(orbitals.shape, f32),
        in_specs=[pl.BlockSpec(memory_space=pltpu.SMEM), pl.BlockSpec(memory_space=pl.ANY)],
        out_specs=pl.BlockSpec(memory_space=pltpu.VMEM),
        scratch_shapes=[
            fine(8), fine(8), vmem((8, 128), f32), vmem((8, 128), f32),
            fine(14), fine(14), fine(12), fine(10), fine(8),
            vmem((10, 24, 128), f32), vmem((6, ROWS1, 128), f32), vmem((8, 24, 128), f32), vmem((6, 32, 128), f32),
            vmem((2, 3, 24, 128), f32), vmem((2, 3, 24, 128), f32),
            vmem((2 * 18 * MSG, 128), f32), vmem((24 * MSG, 128), f32),
            fine(8), fine(8),
            dma, dma((2,)), dma((2,)), dma((2,)), dma((2,)), dma((2,)), dma((4,)), dma((4,)), dma((2,)), dma((2,)), dma((4,)), dma((4,)),
        ],
        compiler_params=pltpu.CompilerParams(collective_id=0, has_side_effects=True, vmem_limit_bytes=32 * 2**20),
    )(occupations, orbitals)


def solution(mesh):
    return jax.shard_map(
        functools.partial(on_device, mesh.shape["orb"], mesh.shape["slab"]),
        mesh=mesh,
        in_specs=(P("orb", "slab", None, None), P("orb")),
        out_specs=P("orb", "slab", None, None),
        check_vma=False,
    )
```

time: 396 us -> 31.8 us (0.08)
  the two profiles are of different devices: /device:TPU:24 before, /device:TPU:2 now
where the time goes in v1:
time: 31.8 us; the launch traced here: 31.7 us
  Pallas kernels  29.4 us (92%)
  local copies, waits for them, and re-layouts  1.6 us (5%)
  between operations  0.67 us (2%)
    pallas_call x1, Pallas kernels, on_device(): pl.pallas_call(functools.partial(kernel, n_orb, n_slab), out_shape=jax.Sh...  29.4 us
    unnamed x3, local copies, waits for them, and re-layouts  1.6 us

profile of v1, /device:TPU:2, one launch (start us, length us, event | category | flops | bytes accessed | tf_op | source)
XLA Modules:
  0.0 31.7 jit_solution(3845348171831722666)
XLA Ops:
  0.7 0.0 copy-start
  0.7 0.9 %copy-done = f32[1,8,48,128]{3,2,1,0:T(8,128)S(1)} copy-done((f32[1,8,48,128]{3,2,1,0:T(8,128)S(1)}, f32[1,8,48,128]{3,2,1,0:T(8,128)}, u32[]{:S(2)}) %copy-start) | copy-done | bytes 196632
  1.6 29.4 %shard_map.28 = f32[1,8,48,128]{3,2,1,0:T(8,128)S(1)} custom-call(f32[1]{0:T(128)S(6)} %copy.4.occ_ref, f32[1,8,48,128]{3,2,1,0:T(8,128)S(1)} %copy-done), custom_call_target="tpu_custom_call" | custom-call | tf_op jit(solution)/shard_map/pallas_call | solution.py:354
  31.0 0.7 %copy.5 = f32[1,8,48,128]{3,2,1,0:T(8,128)} copy(f32[1,8,48,128]{3,2,1,0:T(8,128)S(1)} %shard_map.28) | data formatting | bytes 393216
Async XLA Ops:
  0.7 0.9 %copy-start = (f32[1,8,48,128]{3,2,1,0:T(8,128)S(1)}, f32[1,8,48,128]{3,2,1,0:T(8,128)}, u32[]{:S(2)}) copy-start(f32[1,8,48,128]{3,2,1,0:T(8,128)} %orb_ref.1) | copy-start | bytes 589828
